TPU v7x, 32 devices: a whole 2x2x4 slice. The times are simulated.
32 devices in a mesh: tok: 8 (over z, x), exp: 4 (over y, core).
Axes of the slice: x: 2, y: 2, z: 4, core: 2. Of those that a mesh axis runs over, the one named last changes fastest.
Arguments:
- tokens_x: bfloat16 [1280, 4096], P('tok', 'exp'), may hold values from -6 to 6
- out_grad: bfloat16 [1280, 4096], P('tok', 'exp'), may hold values from -12 to 12
- expert_ids: int32 [1280, 8], P('tok'), may hold values from 0 to 31, as said below
- route_q: int32 [1280, 8], P('tok'), may hold values from 1 to 255
- gate_w: bfloat16 [4, 1536, 4096], P('exp', 'tok'), may hold values from -0.09375 to 0.09375
- up_w: bfloat16 [4, 1536, 4096], P('exp', 'tok'), may hold values from -0.09375 to 0.09375
- down_w: bfloat16 [4, 1536, 4096], P('exp', 'tok'), may hold values from -0.15625 to 0.15625
Outputs:
- input_factor: float32 [4, 4096, 4096], P('exp', 'tok')
- grad_factor: float32 [4, 1536, 1536], P('exp', 'tok')
Inputs may be any that keep to these rules, and one draw needn't show every extreme that they name: `expert_ids`: each token names exactly one expert from each range of 4 ids that starts at a multiple of 4, in varying positions of its row. Within the rows of one index of tok (aligned blocks of 160 rows) no expert below 4 is named by more than 80 rows, and in every draw one expert below 4 is named by exactly 80 rows in every block.
All inputs are finite; a program needn't handle non-finite values.
Results may differ from a plain program's by a relative error of at most 0.0056.
Values may be sent and summed in bfloat16 or wider, within the bound.
A program may use at most 64 MiB of HBM per device.

v0:
```python
import jax
import jax.numpy as jnp
from jax import lax
from jax.sharding import PartitionSpec as P


def silu_slope(values):
    sigma = jax.nn.sigmoid(values)
    return sigma * (1.0 + values * (1.0 - sigma))


def local(tokens_x, out_grad, expert_ids, route_q, gate_w, up_w, down_w):
    owners = lax.axis_size("exp")
    shards = lax.axis_size("tok")
    position = lax.axis_index("tok")
    tok_rows = tokens_x.shape[0]
    local_width = tokens_x.shape[1]
    capacity = 2 * tok_rows // owners
    slot_count = capacity * shards
    fitted = expert_ids < owners
    fitted_id = jnp.sum(jnp.where(fitted, expert_ids, 0), axis=1)
    route_weight = jnp.sum(jnp.where(fitted, route_q, 0), axis=1).astype(jnp.float32) / 256.0
    onehot = (fitted_id[:, None] == jnp.arange(owners, dtype=jnp.int32)[None, :]).astype(jnp.int32)
    running = jnp.cumsum(onehot, axis=0)
    rank_in = jnp.sum(running * onehot, axis=1) - 1
    slot_ids = fitted_id * capacity + rank_in
    packer = (slot_ids[None, :] == jnp.arange(owners * capacity, dtype=jnp.int32)[:, None]).astype(
        jnp.bfloat16
    )
    scaled = (route_weight[:, None] * out_grad.astype(jnp.float32)).astype(jnp.bfloat16)
    packed_x = jnp.dot(packer, tokens_x, preferred_element_type=jnp.float32).astype(jnp.bfloat16)
    packed_g = jnp.dot(packer, scaled, preferred_element_type=jnp.float32).astype(jnp.bfloat16)
    packed_x = packed_x.reshape(owners, capacity, local_width)
    packed_g = packed_g.reshape(owners, capacity, local_width)
    recv_x, recv_g = (
        lax.all_to_all(packed_x, "exp", split_axis=0, concat_axis=2, tiled=True),
        lax.all_to_all(packed_g, "exp", split_axis=0, concat_axis=2, tiled=True),
    )
    full_width = local_width * owners
    x_slots = recv_x.reshape(capacity, full_width)
    g_slots = recv_g.reshape(capacity, full_width)
    w_gate = gate_w[0]
    w_up = up_w[0]
    w_down = down_w[0]
    contract = (((1,), (1,)), ((), ()))
    x_piece = lax.all_gather(x_slots, "tok", axis=0, tiled=True)
    g_piece = lax.all_gather(g_slots, "tok", axis=0, tiled=True)
    gate_pre = lax.dot_general(w_gate, x_piece, contract, preferred_element_type=jnp.float32)
    up_pre = lax.dot_general(w_up, x_piece, contract, preferred_element_type=jnp.float32)
    hidden_grad = lax.dot_general(w_down, g_piece, contract, preferred_element_type=jnp.float32)
    gate_grad = (hidden_grad * up_pre * silu_slope(gate_pre)).astype(jnp.bfloat16)
    all_rows = x_piece
    all_rows, grad_cols = (all_rows, gate_grad)
    strip_width = full_width // shards
    column_strip = lax.dynamic_slice_in_dim(all_rows, position * strip_width, strip_width, 1)
    input_rows = lax.dot_general(
        column_strip, all_rows, (((0,), (0,)), ((), ())), preferred_element_type=jnp.float32
    )
    input_rows = input_rows / float(slot_count)
    grad_rows = lax.dot_general(
        grad_cols,
        lax.all_gather(grad_cols, "tok", axis=0, tiled=True),
        contract,
        preferred_element_type=jnp.float32,
    )
    grad_rows = grad_rows / float(slot_count)
    return (input_rows[None], grad_rows[None])


def solution(mesh):
    placed = (
        P("tok", "exp"),
        P("tok", "exp"),
        P("tok", None),
        P("tok", None),
        P("exp", "tok", None),
        P("exp", "tok", None),
        P("exp", "tok", None),
    )
    return jax.shard_map(
        local,
        mesh=mesh,
        in_specs=placed,
        out_specs=(P("exp", "tok", None), P("exp", "tok", None)),
        check_vma=False,
    )
```

profile of v0, /device:TPU:0, one launch (start us, length us, event | category | flops | bytes accessed | tf_op | source)
XLA Modules:
  0.0 262.4 jit_solution(2773389394463155774)
XLA Ops:
  7.2 0.8 fusion.27
  8.1 1.2 reduce-window.6
  9.3 0.1 slice.12
  9.4 0.1 copy.15
  9.6 0.1 copy.16
  9.6 0.1 add_bitcast_fusion
  9.8 1.3 convolution_convert_fusion.1
  11.1 14.3 %all_to_all.30 = bf16[4,80,1024]{2,1,0:T(8,128)(2,1)S(1)} all-to-all(bf16[4,80,1024]{2,1,0:T(8,128)(2,1)S(1)} %bitcast.68), channel_id=1, replica_groups=mesh['tok'=8,'exp'=4] {'exp'}, dimensions={0} | all-to-all | bytes 1310720 | tf_op jit(solution)/shard_map/all_to_all | solution.py:36
  25.4 0.5 copy.17
  25.9 1.1 copy.20
  27.0 0.0 all-gather.6.cloned.1.call-start
  27.0 0.4 convolution_convert_fusion
  27.4 12.7 %all_to_all.31 = bf16[4,80,1024]{2,1,0:T(8,128)(2,1)S(1)} all-to-all(bf16[4,80,1024]{2,1,0:T(8,128)(2,1)S(1)} %bitcast.63), channel_id=1, replica_groups=mesh['tok'=8,'exp'=4] {'exp'}, dimensions={0} | all-to-all | bytes 1310720 | tf_op jit(solution)/shard_map/all_to_all | solution.py:37
  40.1 0.5 copy.18
  40.6 1.1 copy.21
  41.7 0.0 all-gather.8.cloned.1.call-start
  41.7 71.9 %all-gather.4.cloned.1.call-done = bf16[640,4096]{1,0:T(8,128)(2,1)} async-done(((bf16[80,4096]{1,0:T(8,128)(2,1)}), bf16[640,4096]{1,0:T(8,128)(2,1)}) %all-gather.4.cloned.1.call-update) | async-done | bytes 5242896 | tf_op jit(solution)/shard_map/all_gather | solution.py:46
  113.7 5.3 %fusion.3 = f32[640,192]{0,1:T(8,128)} fusion(bf16[640,4096]{1,0:T(8,128)(2,1)} %all-gather.4.cloned.1.call-done, bf16[1,192,4096]{2,1,0:T(8,128)(2,1)S(1)} %copy-done), kind=kOutput, calls=%fused_computation.5 | convolution fusion | flops 1006632960 | bytes 7307264 | tf_op jit(solution)/shard_map/dot_general | solution.py:49
  119.0 2.8 %fusion.13 = f32[192,640]{1,0:T(8,128)} fusion(bf16[640,4096]{1,0:T(8,128)(2,1)S(1)} %copy-done.1, bf16[1,192,4096]{2,1,0:T(8,128)(2,1)S(1)} %copy-done.4), kind=kOutput, calls=%fused_computation.13 | convolution fusion | flops 1006632960 | bytes 7307264 | tf_op jit(solution)/shard_map/dot_general | solution.py:48
  121.7 79.2 %all-gather.6.cloned.1.call-done = bf16[640,4096]{1,0:T(8,128)(2,1)} async-done(((bf16[80,4096]{1,0:T(8,128)(2,1)}), bf16[640,4096]{1,0:T(8,128)(2,1)}) %all-gather.6.cloned.1.call-update) | async-done | bytes 5242896 | tf_op jit(solution)/shard_map/all_gather | solution.py:47
  200.9 5.7 %fusion.19 = bf16[192,640]{1,0:T(8,128)(2,1)} fusion(f32[640,192]{0,1:T(8,128)} %fusion.3, bf16[640,4096]{1,0:T(8,128)(2,1)} %all-gather.6.cloned.1.call-done, bf16[1,192,4096]{2,1,0:T(8,128)(2,1)} %param.13, f32[192,640]{1,0:T(8,128)} %fusion.13), kind=kOutput, calls=%fused_computation.15 | convolution fusion | flops 1007861760 | bytes 8044544 | tf_op jit(solution)/shard_map/dot_general | solution.py:50
  206.7 9.6 %multiply_bitcast_fusion = f32[1,512,4096]{2,1,0:T(8,128)} fusion(bf16[640,4096]{1,0:T(8,128)(2,1)} %all-gather.4.cloned.1.call-done, s32[]{:T(128)S(6)} %select_n.11), kind=kOutput, calls=%fused_computation | convolution fusion | flops 2686451712 | bytes 14286852 | tf_op jit(solution)/shard_map/dot_general | solution.py:56
  216.3 36.2 %all-gather.8.cloned.1.call-done = bf16[1536,640]{1,0:T(8,128)(2,1)} async-done(((bf16[192,640]{1,0:T(8,128)(2,1)}), bf16[1536,640]{1,0:T(8,128)(2,1)}) %all-gather.8.cloned.1.call-update) | async-done | bytes 1966096 | tf_op jit(solution)/shard_map/all_gather | solution.py:62
  252.5 3.4 %fusion = f32[1,192,1536]{2,1,0:T(8,128)} fusion(bf16[192,640]{1,0:T(8,128)(2,1)S(1)} %copy-done.2, bf16[1536,640]{1,0:T(8,128)(2,1)} %all-gather.8.cloned.1.call-done), kind=kOutput, calls=%fused_computation.2 | convolution fusion | flops 377782272 | bytes 3391488 | tf_op jit(solution)/shard_map/dot_general | solution.py:60
  (23 shorter events, 0.2 us)
Async XLA Ops:
  7.2 106.5 %copy-start = (bf16[1,192,4096]{2,1,0:T(8,128)(2,1)S(1)}, bf16[1,192,4096]{2,1,0:T(8,128)(2,1)}, u32[]{:S(2)}) copy-start(bf16[1,192,4096]{2,1,0:T(8,128)(2,1)} %param.12) | copy-start | bytes 4718596
  7.2 106.5 %all-gather.4.cloned.1.call-start = ((), (), s32[]{:S(2)}) async-start(), calls=%async_computation.2 | async-start | bytes 5898240 | tf_op jit(solution)/shard_map/all_gather | solution.py:46
  25.4 1.7 copy-start.3
  27.0 173.9 %all-gather.6.cloned.1.call-start = ((), (), s32[]{:S(2)}) async-start(), calls=%async_computation.3 | async-start | bytes 5898240 | tf_op jit(solution)/shard_map/all_gather | solution.py:47
  41.7 77.3 %copy-start.4 = (bf16[1,192,4096]{2,1,0:T(8,128)(2,1)S(1)}, bf16[1,192,4096]{2,1,0:T(8,128)(2,1)}, u32[]{:S(2)}) copy-start(bf16[1,192,4096]{2,1,0:T(8,128)(2,1)} %param.11) | copy-start | bytes 4718596
  41.7 210.8 %all-gather.8.cloned.1.call-start = ((), (), s32[]{:S(2)}) async-start(), calls=%async_computation.4 | async-start | bytes 2211840 | tf_op jit(solution)/shard_map/all_gather | solution.py:62
  113.7 5.3 %copy-start.1 = (bf16[640,4096]{1,0:T(8,128)(2,1)S(1)}, bf16[640,4096]{1,0:T(8,128)(2,1)}, u32[]{:S(2)}) copy-start(bf16[640,4096]{1,0:T(8,128)(2,1)} %all-gather.4.cloned.1.call-done) | copy-start | bytes 15728644
  206.6 45.8 %copy-start.2 = (bf16[192,640]{1,0:T(8,128)(2,1)S(1)}, bf16[192,640]{1,0:T(8,128)(2,1)}, u32[]{:S(2)}) copy-start(bf16[192,640]{1,0:T(8,128)(2,1)} %fusion.19) | copy-start | bytes 737284
Sparse Core Ops, SparseCore 0:
  27.1 86.5 all-gather.3
  116.4 84.4 all-gather.5
  206.8 45.6 all-gather.7
where the time goes:
time: 263 us; the launch traced here: 262 us
  waiting for transfers between devices  187 us (71%)
  matrix products  28.5 us (11%)
  blocking collectives  26.9 us (10%)
  between operations  13.8 us (5%)
  local copies, waits for them, and re-layouts  3.45 us (1%)
    all_gather x1, waiting for transfers between devices, local(): g_piece = lax.all_gather(g_slots, 'tok', axis=0, tiled=True)  79.2 us
    all_gather x1, waiting for transfers between devices, local(): x_piece = lax.all_gather(x_slots, 'tok', axis=0, tiled=True)  71.9 us
    all_gather x1, waiting for transfers between devices, local(): lax.all_gather(grad_cols, 'tok', axis=0, tiled=True)  36.2 us
    all_to_all x1, blocking collectives, local(): lax.all_to_all(packed_x, 'exp', split_axis=0, concat_axis=2, tiled=True)  14.3 us
    all_to_all x1, blocking collectives, local(): lax.all_to_all(packed_g, 'exp', split_axis=0, concat_axis=2, tiled=True)  12.7 us
    dot_general x1, matrix products, local(): lax.dot_general(column_strip, all_rows, (((0,), (0,)), ((), ())), preferr...  9.62 us
    dot_general x1, matrix products, local(): lax.dot_general(w_down, g_piece, contract, preferred_element_type=jnp.flo...  5.72 us
    dot_general x1, matrix products, local(): lax.dot_general(w_up, x_piece, contract, preferred_element_type=jnp.float32)  5.28 us
  transfers between devices with their start and end apart: 3, of which 3 were waited for; matrix products, arithmetic and copies ran while one was open for 7% of the time, Pallas kernels for 0%

commit v1 on v0

v1 whole, which is shorter than its diff:
```python
import functools

import jax
import jax.numpy as jnp
from jax import lax
from jax.experimental import pallas as pl
from jax.experimental.pallas import tpu as pltpu
from jax.sharding import PartitionSpec as P

MESH = pl.DeviceIdType.MESH
NT = (((1,), (1,)), ((), ()))


def silu_slope(values):
    sigma = jax.nn.sigmoid(values)
    return sigma * (1.0 + values * (1.0 - sigma))


def ring_place(index, count):
    odd = lax.rem(index, 2)
    half = index // 2
    return (1 - odd) * half + odd * (count - 1 - half)


def ring_index(place, count):
    place = lax.rem(place + 2 * count, count)
    late = place // (count // 2)
    return (1 - late) * (2 * place) + late * (2 * (count - 1 - place) + 1)


def exchange_kernel(
    shards, owners,
    px_ref, pg_ref, wg_ref, wu_ref, wd_ref,
    x_out, gg_out,
    xbuf, gbuf, wg, wu, wd, acc, factor, gg,
    swap_send, swap_recv, own_sem, ring_send, ring_recv, gg_send, gg_recv, load_sem, store_sem,
):
    tok = lax.axis_index("tok")
    exp = lax.axis_index("exp")
    place = ring_place(tok, shards)
    ahead = ring_index(place + 1, shards)
    behind = ring_index(place - 1, shards)
    width = px_ref.shape[2]
    full = xbuf.shape[2]
    cap = xbuf.shape[1]
    far = shards // 2
    near = (shards - 1) // 2

    barrier = pltpu.get_barrier_semaphore()
    for neighbour in (ahead, behind):
        pl.semaphore_signal(barrier, inc=1, device_id=(neighbour, exp), device_id_type=MESH)
    for k in range(1, owners):
        pl.semaphore_signal(
            barrier, inc=1, device_id=(tok, lax.rem(exp + k, owners)), device_id_type=MESH
        )
    pl.semaphore_wait(barrier, owners + 1)

    sent = []
    columns = pl.ds(pl.multiple_of(exp * width, 128), width)
    swaps = [[], []]
    for a, (packed, buf) in enumerate(((px_ref, xbuf), (pg_ref, gbuf))):
        for k in range(1, owners):
            peer = lax.rem(exp + k, owners)
            copy = pltpu.make_async_remote_copy(
                src_ref=packed.at[peer],
                dst_ref=buf.at[tok, :, columns],
                send_sem=swap_send.at[a, k],
                recv_sem=swap_recv.at[a, k],
                device_id=(tok, peer),
                device_id_type=MESH,
            )
            copy.start()
            sent.append(copy)
            swaps[a].append(copy)
        own = pltpu.make_async_copy(packed.at[exp], buf.at[tok, :, columns], own_sem.at[a])
        own.start()
        swaps[a].append(own)

    loads = []
    for i, (src, dst) in enumerate(((wg_ref, wg), (wu_ref, wu), (wd_ref, wd))):
        load = pltpu.make_async_copy(src, dst, load_sem.at[i])
        load.start()
        loads.append(load)

    def finish_swap(a):
        for copy in swaps[a][:-1]:
            copy.wait_recv()
        swaps[a][-1].wait()

    half = full // 2
    bufs = (xbuf, gbuf)
    copies = {}

    def send(a, d, hop, c):
        block = ring_index(place - hop if d == 0 else place + hop, shards)
        view = bufs[a].at[block, :, pl.ds(c * half, half)]
        copy = pltpu.make_async_remote_copy(
            src_ref=view,
            dst_ref=view,
            send_sem=ring_send.at[a, d, hop, c],
            recv_sem=ring_recv.at[a, d, hop, c],
            device_id=(ahead if d == 0 else behind, exp),
            device_id_type=MESH,
        )
        copy.start()
        sent.append(copy)
        copies[a, d, hop, c] = copy

    def product(weights, buf):
        rows = buf.shape[0] * cap
        step = min(1024, full)
        acc[...] = jnp.zeros_like(acc)

        def body(i, carry):
            part = pl.ds(pl.multiple_of(i * step, step), step)
            acc[...] += lax.dot_general(
                weights[:, part],
                buf[:, :, part].reshape(rows, step),
                NT,
                preferred_element_type=jnp.float32,
            )
            return carry

        lax.fori_loop(0, full // step, body, 0)

    orders = (
        [(0, h) for h in range(far)] + [(1, h) for h in range(near)],
        [(0, h) for h in range(near)] + [(1, h) for h in range(far)],
    )
    swapped = set()
    store_x = pltpu.make_async_copy(xbuf, x_out, store_sem.at[0])
    for s in range(far + near):
        for c in range(2):
            for d in range(2):
                a, hop = orders[d][s]
                if hop == 0:
                    if a not in swapped:
                        finish_swap(a)
                        swapped.add(a)
                else:
                    copies[a, d, hop - 1, c].wait_recv()
                send(a, d, hop, c)
        if s == far:
            for c in range(2):
                copies[0, 0, far - 1, c].wait_recv()
                copies[0, 1, near - 1, c].wait_recv()
            store_x.start()
            loads[0].wait()
            product(wg, xbuf)
            factor[...] = silu_slope(acc[...])
        if s == far + 1:
            loads[1].wait()
            product(wu, xbuf)
            factor[...] = factor[...] * acc[...]

    for c in range(2):
        copies[1, 0, near - 1, c].wait_recv()
        copies[1, 1, far - 1, c].wait_recv()
    loads[2].wait()
    product(wd, gbuf)
    gg[tok] = (acc[...] * factor[...]).astype(gg.dtype)

    units = gg.shape[1]
    first = -(-(units // 2) // 16) * 16
    cuts = (pl.ds(0, first), pl.ds(first, units - first))
    gg_copies = {}
    for hop in range(far):
        for c in range(2):
            for d in range(2):
                if hop >= near and c != d:
                    continue
                if hop > 0:
                    gg_copies[d, hop - 1, c].wait_recv()
                block = ring_index(place - hop if d == 0 else place + hop, shards)
                view = gg.at[block, cuts[c], :]
                copy = pltpu.make_async_remote_copy(
                    src_ref=view,
                    dst_ref=view,
                    send_sem=gg_send.at[d, hop, c],
                    recv_sem=gg_recv.at[d, hop, c],
                    device_id=(ahead if d == 0 else behind, exp),
                    device_id_type=MESH,
                )
                copy.start()
                sent.append(copy)
                gg_copies[d, hop, c] = copy
    for (d, hop, c), copy in gg_copies.items():
        if (d, hop + 1, c) not in gg_copies:
            copy.wait_recv()
    store_gg = pltpu.make_async_copy(gg, gg_out, store_sem.at[1])
    store_gg.start()
    for copy in sent:
        copy.wait_send()
    store_x.wait()
    store_gg.wait()


def local(tokens_x, out_grad, expert_ids, route_q, gate_w, up_w, down_w):
    owners = lax.axis_size("exp")
    shards = lax.axis_size("tok")
    position = lax.axis_index("tok")
    tok_rows = tokens_x.shape[0]
    local_width = tokens_x.shape[1]
    capacity = 2 * tok_rows // owners
    slot_count = capacity * shards
    padded = -(-capacity // 16) * 16
    fitted = expert_ids < owners
    fitted_id = jnp.sum(jnp.where(fitted, expert_ids, 0), axis=1)
    route_weight = jnp.sum(jnp.where(fitted, route_q, 0), axis=1).astype(jnp.float32) / 256.0
    order = jnp.arange(tok_rows, dtype=jnp.int32)
    earlier = (fitted_id[:, None] == fitted_id[None, :]) & (order[:, None] > order[None, :])
    rank_in = jnp.sum(earlier.astype(jnp.int32), axis=1)
    slot_ids = fitted_id * padded + rank_in
    packer = (slot_ids[None, :] == jnp.arange(owners * padded, dtype=jnp.int32)[:, None]).astype(
        jnp.bfloat16
    )
    scaled = (route_weight[:, None] * out_grad.astype(jnp.float32)).astype(jnp.bfloat16)
    packed_x = jnp.dot(packer, tokens_x, preferred_element_type=jnp.float32).astype(jnp.bfloat16)
    packed_g = jnp.dot(packer, scaled, preferred_element_type=jnp.float32).astype(jnp.bfloat16)
    packed_x = packed_x.reshape(owners, padded, local_width)
    packed_g = packed_g.reshape(owners, padded, local_width)
    full_width = local_width * owners
    units = gate_w.shape[1]
    rows = shards * padded
    far = shards // 2
    vmem = pl.BlockSpec(memory_space=pltpu.VMEM)
    anywhere = pl.BlockSpec(memory_space=pl.ANY)
    dma = pltpu.SemaphoreType.DMA
    x_all, gg_all = pl.pallas_call(
        functools.partial(exchange_kernel, shards, owners),
        out_shape=(
            jax.ShapeDtypeStruct((shards, padded, full_width), jnp.bfloat16),
            jax.ShapeDtypeStruct((shards, units, rows), jnp.bfloat16),
        ),
        in_specs=[vmem, vmem, anywhere, anywhere, anywhere],
        out_specs=(anywhere, anywhere),
        scratch_shapes=[
            pltpu.VMEM((shards, padded, full_width), jnp.bfloat16),
            pltpu.VMEM((shards, padded, full_width), jnp.bfloat16),
            pltpu.VMEM((units, full_width), jnp.bfloat16),
            pltpu.VMEM((units, full_width), jnp.bfloat16),
            pltpu.VMEM((units, full_width), jnp.bfloat16),
            pltpu.VMEM((units, rows), jnp.float32),
            pltpu.VMEM((units, rows), jnp.float32),
            pltpu.VMEM((shards, units, rows), jnp.bfloat16),
            dma((2, owners)),
            dma((2, owners)),
            dma((2,)),
            dma((2, 2, far, 2)),
            dma((2, 2, far, 2)),
            dma((2, far, 2)),
            dma((2, far, 2)),
            dma((3,)),
            dma((2,)),
        ],
        compiler_params=pltpu.CompilerParams(
            collective_id=0, has_side_effects=True, vmem_limit_bytes=48 * 2**20
        ),
        cost_estimate=pl.CostEstimate(
            flops=6 * units * rows * full_width,
            bytes_accessed=20 * 2**20,
            transcendentals=units * rows,
        ),
    )(packed_x, packed_g, gate_w[0], up_w[0], down_w[0])
    all_rows = x_all.reshape(rows, full_width)
    strip_width = full_width // shards
    column_strip = lax.dynamic_slice_in_dim(all_rows, position * strip_width, strip_width, 1)
    input_rows = lax.dot_general(
        column_strip, all_rows, (((0,), (0,)), ((), ())), preferred_element_type=jnp.float32
    )
    input_rows = input_rows / float(slot_count)
    grad_cols = lax.dynamic_index_in_dim(gg_all, position, 0, keepdims=False)
    grad_rows = lax.dot_general(
        grad_cols, gg_all.reshape(shards * units, rows), NT, preferred_element_type=jnp.float32
    )
    grad_rows = grad_rows / float(slot_count)
    return (input_rows[None], grad_rows[None])


def solution(mesh):
    placed = (
        P("tok", "exp"),
        P("tok", "exp"),
        P("tok", None),
        P("tok", None),
        P("exp", "tok", None),
        P("exp", "tok", None),
        P("exp", "tok", None),
    )
    return jax.shard_map(
        local,
        mesh=mesh,
        in_specs=placed,
        out_specs=(P("exp", "tok", None), P("exp", "tok", None)),
        check_vma=False,
    )
```

time: 263 us -> 155 us (0.59)
  waiting for transfers between devices: 187 us -> 0 us
  Pallas kernels: 0 us -> 134 us
  blocking collectives: 26.9 us -> 0 us
  matrix products: 28.5 us -> 14.8 us
  between operations: 13.8 us -> 0.71 us
    all_gather x3 -> x0, waiting for transfers between devices: 187 us -> none  [the longest x1 79.2 us: local(): g_piece = lax.all_gather(g_slots, 'tok', axis=0, tiled=True)]
    pallas_call x0 -> x1, Pallas kernels: none -> 134 us  [local(): pl.pallas_call(functools.partial(exchange_kernel, shards, owners), out_sh...]
    all_to_all x2 -> x0, blocking collectives: 26.9 us -> none  [the longest x1 14.3 us: local(): lax.all_to_all(packed_x, 'exp', split_axis=0, concat_axis=2, tiled=True)]
    dot_general x4 -> x1, matrix products: 17.1 us -> 3.53 us  [local(): lax.dot_general(grad_cols, gg_all.reshape(shards * units, rows), NT, pref...]
  transfers between devices with their start and end apart: 3 -> 0, of which waited for: 3 -> 0; matrix products, arithmetic and copies ran while one was open for 7% -> 0% of each run, Pallas kernels for 0% -> 0%
where the time goes in v1:
time: 155 us; the launch traced here: 154 us
  Pallas kernels  134 us (86%)
  matrix products  14.8 us (10%)
  local copies, waits for them, and re-layouts  2.82 us (2%)
    pallas_call x1, Pallas kernels, local(): pl.pallas_call(functools.partial(exchange_kernel, shards, owners), out_sh...  134 us
    dot_general x1, matrix products, local(): lax.dot_general(column_strip, all_rows, (((0,), (0,)), ((), ())), preferr...  9.58 us
    dot_general x1, matrix products, local(): lax.dot_general(grad_cols, gg_all.reshape(shards * units, rows), NT, pref...  3.53 us

profile of v1, /device:TPU:0, one launch (start us, length us, event | category | flops | bytes accessed | tf_op | source)
XLA Modules:
  0.0 153.7 jit_solution(80756429359958395)
XLA Ops:
  0.6 0.0 copy-start
  0.6 0.0 copy-start.1
  0.7 0.9 fusion.9
  1.5 0.2 convert_reduce_fusion
  1.7 1.4 convolution_convert_fusion
  3.1 0.0 copy-done
  3.1 0.3 convolution_convert_fusion.1
  3.5 0.0 copy-done.1
  3.5 0.0 copy-start.2
  3.5 1.4 copy-done.2
  4.9 0.0 copy-start.3
  4.9 1.4 copy-done.3
  6.3 134.3 %shard_map.86 = (bf16[8,80,4096]{2,1,0:T(8,128)(2,1)}, bf16[8,192,640]{2,1,0:T(8,128)(2,1)}) custom-call(bf16[4,80,1024]{2,1,0:T(8,128)(2,1)S(1)} %bitcast.17, bf16[4,80,1024]{2,1,0:T(8,128)(2,1)S(1)} %bitcast.18, bf16[192,4096]{1,0:T(8,128)(2,1)S(1)} %bitcast.19, bf16[192,4096]{1,0:T(8,128)(2,1)S(1)} %bitcast.20, bf16[192,4096]{1,0:T(8,128)(2,1)S(1)} %bitcast.21), custom_call_target="tpu_custom_call" | custom-call | flops 3019898880 | bytes 20971520 | tf_op jit(solution)/shard_map/pallas_call | solution.py:229
  140.6 3.5 %fusion = f32[1,192,1536]{2,1,0:T(8,128)} fusion(bf16[1536,640]{1,0:T(8,128)(2,1)} %bitcast.23, bf16[8,192,640]{2,1,0:T(8,128)(2,1)} %get-tuple-element.5, s32[]{:T(128)S(6)} %select_n.17), kind=kOutput, calls=%fused_computation.2 | convolution fusion | flops 377782272 | bytes 3391492 | tf_op jit(solution)/shard_map/dot_general | solution.py:273
  144.2 9.6 %multiply_bitcast_fusion = f32[1,512,4096]{2,1,0:T(8,128)} fusion(bf16[640,4096]{1,0:T(8,128)(2,1)} %bitcast.22, s32[]{:T(128)S(6)} %select_n.16), kind=kOutput, calls=%fused_computation | convolution fusion | flops 2686451712 | bytes 14286852 | tf_op jit(solution)/shard_map/dot_general | solution.py:268
  (2 shorter events, 0.0 us)
Async XLA Ops:
  0.6 2.5 %copy-start = (bf16[160,1024]{1,0:T(8,128)(2,1)S(1)}, bf16[160,1024]{1,0:T(8,128)(2,1)}, u32[]{:S(2)}) copy-start(bf16[160,1024]{1,0:T(8,128)(2,1)} %param.7) | copy-start | bytes 983044
  0.6 2.8 %copy-start.1 = (bf16[1,192,4096]{2,1,0:T(8,128)(2,1)S(1)}, bf16[1,192,4096]{2,1,0:T(8,128)(2,1)}, u32[]{:S(2)}) copy-start(bf16[1,192,4096]{2,1,0:T(8,128)(2,1)} %param.11) | copy-start | bytes 4718596
  3.5 1.4 copy-start.2
  4.9 1.4 copy-start.3

commit v2 on v1

v2 whole, which is shorter than its diff:
```python
import functools

import jax
import jax.numpy as jnp
from jax import lax
from jax.experimental import pallas as pl
from jax.experimental.pallas import tpu as pltpu
from jax.sharding import PartitionSpec as P

MESH = pl.DeviceIdType.MESH
NT = (((1,), (1,)), ((), ()))


def silu_slope(values):
    sigma = jax.nn.sigmoid(values)
    return sigma * (1.0 + values * (1.0 - sigma))


def ring_place(index, count):
    odd = lax.rem(index, 2)
    half = index // 2
    return (1 - odd) * half + odd * (count - 1 - half)


def ring_index(place, count):
    place = lax.rem(place + 2 * count, count)
    late = place // (count // 2)
    return (1 - late) * (2 * place) + late * (2 * (count - 1 - place) + 1)


def exchange_kernel(
    shards, owners, slot_count,
    px_ref, raw_ref, ids_ref, wg_ref, wu_ref, wd_ref,
    in_out, gg_out,
    xbuf, gbuf, raw, packed, ids, wg, wu, wd, acc, factor, gg, strip, wide,
    ids_send, ids_recv, swap_send, swap_recv, own_sem, ring_send, ring_recv,
    gg_send, gg_recv, load_sem, store_sem,
):
    tok = lax.axis_index("tok")
    exp = lax.axis_index("exp")
    place = ring_place(tok, shards)
    ahead = ring_index(place + 1, shards)
    behind = ring_index(place - 1, shards)
    width = px_ref.shape[2]
    full = xbuf.shape[2]
    cap = xbuf.shape[1]
    rows = shards * cap
    far = shards // 2
    near = (shards - 1) // 2

    barrier = pltpu.get_barrier_semaphore()
    for k in range(1, shards):
        pl.semaphore_signal(
            barrier, inc=1, device_id=(lax.rem(tok + k, shards), exp), device_id_type=MESH
        )
    for k in range(1, owners):
        pl.semaphore_signal(
            barrier, inc=1, device_id=(tok, lax.rem(exp + k, owners)), device_id_type=MESH
        )
    pl.semaphore_wait(barrier, shards + owners - 2)

    sent = []

    def remote(src, dst, send_sem, recv_sem, device):
        copy = pltpu.make_async_remote_copy(
            src_ref=src,
            dst_ref=dst,
            send_sem=send_sem,
            recv_sem=recv_sem,
            device_id=device,
            device_id_type=MESH,
        )
        copy.start()
        sent.append(copy)
        return copy

    copies = {}

    def send(a, d, hop, c):
        block = ring_index(place - hop if d == 0 else place + hop, shards)
        buf = (raw, xbuf)[a]
        half = buf.shape[2] // 2
        view = buf.at[block, :, pl.ds(c * half, half)]
        src = raw_ref.at[:, pl.ds(c * half, half)] if a == 0 and hop == 0 else view
        copies[a, d, hop, c] = remote(
            src,
            view,
            ring_send.at[a, d, hop, c],
            ring_recv.at[a, d, hop, c],
            (ahead if d == 0 else behind, exp),
        )

    columns = pl.ds(pl.multiple_of(exp * width, 128), width)
    swaps = []

    def swap(j, source, buf, block):
        for k in range(1, owners):
            peer = lax.rem(exp + k, owners)
            swaps.append((j, remote(
                source(peer),
                buf.at[block, :, columns],
                swap_send.at[j, k],
                swap_recv.at[j, k],
                (tok, peer),
            ).wait_recv))
        own = pltpu.make_async_copy(source(exp), buf.at[block, :, columns], own_sem.at[j])
        own.start()
        swaps.append((j, own.wait))

    slot_iota = lax.broadcasted_iota(jnp.int32, (owners * cap, ids.shape[2]), 0)

    def pack(j, block, tokens):
        picks = (slot_iota == ids[block, 0:1, :]).astype(jnp.float32).astype(jnp.bfloat16)
        chosen = jnp.dot(picks, tokens, preferred_element_type=jnp.float32)
        packed[block] = chosen.astype(jnp.bfloat16).reshape(owners, cap, width)
        swap(j, lambda e: packed.at[block, e], gbuf, block)

    id_copies = []

    orders = (
        [(0, h) for h in range(far)] + [(1, h) for h in range(near)],
        [(0, h) for h in range(near)] + [(1, h) for h in range(far)],
    )
    for c in range(2):
        for d in range(2):
            send(0, d, 0, c)
    ids[tok] = ids_ref[...]
    for k in range(1, shards):
        id_copies.append(remote(
            ids_ref, ids.at[tok], ids_send.at[k], ids_recv.at[k], (lax.rem(tok + k, shards), exp)
        ))
    swap(0, lambda e: px_ref.at[e], xbuf, tok)
    pack(1, tok, raw_ref[...])
    number = 2

    loads = []
    for i, (src, dst) in enumerate(((wd_ref, wd), (wg_ref, wg), (wu_ref, wu))):
        load = pltpu.make_async_copy(src, dst, load_sem.at[i])
        load.start()
        loads.append(load)

    for copy in id_copies:
        copy.wait_recv()

    x_ready = False
    for s in range(1, far + near):
        landed = []
        for c in range(2):
            for d in range(2):
                a, hop = orders[d][s - 1]
                copies[a, d, hop, c].wait_recv()
                if c == 1 and a == 0:
                    landed.append((d, hop + 1))
                if orders[d][s] == (1, 0) and not x_ready:
                    for j, wait in swaps:
                        if j == 0:
                            wait()
                    x_ready = True
                send(*(orders[d][s][0], d, orders[d][s][1], c))
        for d, hop in landed:
            block = ring_index(place - hop if d == 0 else place + hop, shards)
            pack(number, block, raw[block])
            number += 1

    def product(weights, buf):
        step = min(1024, full)
        acc[...] = jnp.zeros_like(acc)

        def body(i, carry):
            part = pl.ds(pl.multiple_of(i * step, step), step)
            acc[...] += lax.dot_general(
                weights[:, part],
                buf[:, :, part].reshape(rows, step),
                NT,
                preferred_element_type=jnp.float32,
            )
            return carry

        lax.fori_loop(0, full // step, body, 0)

    for j, wait in swaps:
        if j > 0:
            wait()
    for load in loads:
        load.wait()
    product(wd, gbuf)
    factor[...] = acc[...]
    for c in range(2):
        for d in range(2):
            copies[1, d, orders[d][-1][1], c].wait_recv()
    product(wu, xbuf)
    factor[...] = factor[...] * acc[...]
    product(wg, xbuf)
    gg[tok] = (factor[...] * silu_slope(acc[...])).astype(gg.dtype)

    tile = min(512, full)
    tiles = full // tile
    strip_width = strip.shape[0]

    def input_tiles(low, high):
        def body(i, carry):
            part = pl.ds(pl.multiple_of(i * tile, tile), tile)
            total = jnp.dot(
                strip[...], xbuf[:, :, part].reshape(rows, tile), preferred_element_type=jnp.float32
            )
            wide[:, part] = total / float(slot_count)
            return carry

        lax.fori_loop(low, high, body, 0)

    units = gg.shape[1]
    first = -(-(units // 2) // 16) * 16
    cuts = (pl.ds(0, first), pl.ds(first, units - first))
    gg_copies = {}
    store_in = pltpu.make_async_copy(wide, in_out, store_sem.at[0])
    for hop in range(far):
        for c in range(2):
            for d in range(2):
                if hop >= near and c != d:
                    continue
                if hop > 0:
                    gg_copies[d, hop - 1, c].wait_recv()
                block = ring_index(place - hop if d == 0 else place + hop, shards)
                view = gg.at[block, cuts[c], :]
                gg_copies[d, hop, c] = remote(
                    view,
                    view,
                    gg_send.at[d, hop, c],
                    gg_recv.at[d, hop, c],
                    (ahead if d == 0 else behind, exp),
                )
        if hop == 0:
            mine = pl.ds(pl.multiple_of(tok * strip_width, 128), strip_width)
            strip[...] = xbuf[:, :, mine].reshape(rows, strip_width).T
            input_tiles(0, tiles // 2)
        if hop == 1:
            input_tiles(tiles // 2, tiles)
            store_in.start()
    for (d, hop, c), copy in gg_copies.items():
        if (d, hop + 1, c) not in gg_copies:
            copy.wait_recv()
    store_gg = pltpu.make_async_copy(gg, gg_out, store_sem.at[1])
    store_gg.start()
    for copy in sent:
        copy.wait_send()
    store_in.wait()
    store_gg.wait()


def local(tokens_x, out_grad, expert_ids, route_q, gate_w, up_w, down_w):
    owners = lax.axis_size("exp")
    shards = lax.axis_size("tok")
    position = lax.axis_index("tok")
    tok_rows = tokens_x.shape[0]
    local_width = tokens_x.shape[1]
    capacity = 2 * tok_rows // owners
    slot_count = capacity * shards
    padded = -(-capacity // 16) * 16
    fitted = expert_ids < owners
    fitted_id = jnp.sum(jnp.where(fitted, expert_ids, 0), axis=1)
    route_weight = jnp.sum(jnp.where(fitted, route_q, 0), axis=1).astype(jnp.float32) / 256.0
    order = jnp.arange(tok_rows, dtype=jnp.int32)
    earlier = (fitted_id[:, None] == fitted_id[None, :]) & (order[:, None] > order[None, :])
    rank_in = jnp.sum(earlier.astype(jnp.int32), axis=1)
    slot_ids = fitted_id * padded + rank_in
    packer = (slot_ids[None, :] == jnp.arange(owners * padded, dtype=jnp.int32)[:, None]).astype(
        jnp.bfloat16
    )
    scaled = (route_weight[:, None] * out_grad.astype(jnp.float32)).astype(jnp.bfloat16)
    packed_x = jnp.dot(packer, tokens_x, preferred_element_type=jnp.float32).astype(jnp.bfloat16)
    packed_x = packed_x.reshape(owners, padded, local_width)
    id_rows = jnp.broadcast_to(slot_ids[None, :], (8, tok_rows))
    full_width = local_width * owners
    units = gate_w.shape[1]
    rows = shards * padded
    far = shards // 2
    vmem = pl.BlockSpec(memory_space=pltpu.VMEM)
    anywhere = pl.BlockSpec(memory_space=pl.ANY)
    dma = pltpu.SemaphoreType.DMA
    input_rows, gg_all = pl.pallas_call(
        functools.partial(exchange_kernel, shards, owners, slot_count),
        out_shape=(
            jax.ShapeDtypeStruct((full_width // shards, full_width), jnp.float32),
            jax.ShapeDtypeStruct((shards, units, rows), jnp.bfloat16),
        ),
        in_specs=[vmem, vmem, vmem, anywhere, anywhere, anywhere],
        out_specs=(anywhere, anywhere),
        scratch_shapes=[
            pltpu.VMEM((shards, padded, full_width), jnp.bfloat16),
            pltpu.VMEM((shards, padded, full_width), jnp.bfloat16),
            pltpu.VMEM((shards, tok_rows, local_width), jnp.bfloat16),
            pltpu.VMEM((shards, owners, padded, local_width), jnp.bfloat16),
            pltpu.VMEM((shards, 8, tok_rows), jnp.int32),
            pltpu.VMEM((units, full_width), jnp.bfloat16),
            pltpu.VMEM((units, full_width), jnp.bfloat16),
            pltpu.VMEM((units, full_width), jnp.bfloat16),
            pltpu.VMEM((units, rows), jnp.float32),
            pltpu.VMEM((units, rows), jnp.float32),
            pltpu.VMEM((shards, units, rows), jnp.bfloat16),
            pltpu.VMEM((full_width // shards, rows), jnp.bfloat16),
            pltpu.VMEM((full_width // shards, full_width), jnp.float32),
            dma((shards,)),
            dma((shards,)),
            dma((shards + 1, owners)),
            dma((shards + 1, owners)),
            dma((shards + 1,)),
            dma((2, 2, far, 2)),
            dma((2, 2, far, 2)),
            dma((2, far, 2)),
            dma((2, far, 2)),
            dma((3,)),
            dma((2,)),
        ],
        compiler_params=pltpu.CompilerParams(
            collective_id=0, has_side_effects=True, vmem_limit_bytes=56 * 2**20
        ),
        cost_estimate=pl.CostEstimate(
            flops=6 * units * rows * full_width,
            bytes_accessed=20 * 2**20,
            transcendentals=units * rows,
        ),
    )(packed_x, scaled, id_rows, gate_w[0], up_w[0], down_w[0])
    grad_cols = lax.dynamic_index_in_dim(gg_all, position, 0, keepdims=False)
    grad_rows = lax.dot_general(
        grad_cols, gg_all.reshape(shards * units, rows), NT, preferred_element_type=jnp.float32
    )
    grad_rows = grad_rows / float(slot_count)
    return (input_rows[None], grad_rows[None])


def solution(mesh):
    placed = (
        P("tok", "exp"),
        P("tok", "exp"),
        P("tok", None),
        P("tok", None),
        P("exp", "tok", None),
        P("exp", "tok", None),
        P("exp", "tok", None),
    )
    return jax.shard_map(
        local,
        mesh=mesh,
        in_specs=placed,
        out_specs=(P("exp", "tok", None), P("exp", "tok", None)),
        check_vma=False,
    )
```

time: 155 us -> 135 us (0.87)
  Pallas kernels: 134 us -> 118 us
  matrix products: 14.8 us -> 4.7 us
  local copies, waits for them, and re-layouts: 2.82 us -> 8.39 us
  other arithmetic: 1.06 us -> 2.79 us
    pallas_call x1, Pallas kernels: 134 us -> 118 us  [local(): pl.pallas_call(functools.partial(exchange_kernel, shards, owners, slot_co...]
    dot_general x2 -> x0, matrix products: 11 us -> none  [the longest x1 9.58 us: local(): lax.dot_general(column_strip, all_rows, (((0,), (0,)), ((), ())), preferr...]
    unnamed x8 -> x3, local copies, waits for them, and re-layouts: 2.82 us -> 7.79 us
    convert_element_type x0 -> x1, other arithmetic: none -> 1.82 us  [local(): (route_weight[:, None] * out_grad.astype(jnp.float32)).astype(jnp.bfloat16)]
where the time goes in v2:
time: 135 us
  Pallas kernels  118 us (87%)
  local copies, waits for them, and re-layouts  8.39 us (6%)
  matrix products  4.7 us (3%)
  other arithmetic  2.79 us (2%)
    pallas_call x1, Pallas kernels, local(): pl.pallas_call(functools.partial(exchange_kernel, shards, owners, slot_co...  118 us
    unnamed x3, local copies, waits for them, and re-layouts  7.79 us
    dot_general x1, matrix products, local(): lax.dot_general(grad_cols, gg_all.reshape(shards * units, rows), NT, pref...  3.53 us

profile of v2, /device:TPU:0, one launch (start us, length us, event | category | flops | bytes accessed | tf_op | source)
XLA Modules:
  0.0 134.8 jit_solution(5422084204040215076)
XLA Ops:
  0.6 0.0 copy-start
  0.6 0.8 fusion.6
  1.4 0.2 convert_reduce_fusion
  1.6 0.0 copy-done
  1.6 1.2 convolution_convert_fusion
  2.8 0.6 broadcast_in_dim.12.ids_ref
  3.4 1.8 %multiply_convert_fusion.raw_ref = bf16[160,1024]{1,0:T(8,128)(2,1)} fusion(bf16[160,1024]{1,0:T(8,128)(2,1)} %param.8, f32[160]{0:T(256)S(1)} %convert_multiply_fusion), kind=kLoop, calls=%fused_computation.3 | loop fusion | flops 491520 | bytes 656000 | tf_op jit(solution)/shard_map/convert_element_type | solution.py:269
  5.2 118.2 %shard_map.86 = (f32[512,4096]{1,0:T(8,128)}, bf16[8,192,640]{2,1,0:T(8,128)(2,1)}) custom-call(bf16[4,80,1024]{2,1,0:T(8,128)(2,1)} %bitcast.15, bf16[160,1024]{1,0:T(8,128)(2,1)} %multiply_convert_fusion.raw_ref, s32[8,160]{1,0:T(8,128)} %broadcast_in_dim.12.ids_ref, bf16[192,4096]{1,0:T(8,128)(2,1)} %bitcast.16, bf16[192,4096]{1,0:T(8,128)(2,1)} %bitcast.17, ...), custom_call_target="tpu_custom_call" | custom-call | flops 3019898880 | bytes 20971520 | tf_op jit(solution)/shard_map/pallas_call | solution.py:280
  123.5 3.5 %fusion = f32[1,192,1536]{2,1,0:T(8,128)} fusion(bf16[1536,640]{1,0:T(8,128)(2,1)} %bitcast.14, bf16[8,192,640]{2,1,0:T(8,128)(2,1)} %get-tuple-element.5, s32[]{:T(128)S(6)} %select_n.13), kind=kOutput, calls=%fused_computation.1 | convolution fusion | flops 377782272 | bytes 3391492 | tf_op jit(solution)/shard_map/dot_general | solution.py:324
  127.0 7.8 %copy.10 = f32[1,512,4096]{2,1,0:T(8,128)} copy(f32[1,512,4096]{2,1,0:T(8,128)} %bitcast.13) | data formatting | bytes 16777216
  (2 shorter events, 0.0 us)
Async XLA Ops:
  0.6 1.0 copy-start

commit v3 on v2

--- a/solution.py
+++ b/solution.py
@@ -30,9 +30,9 @@
 
 def exchange_kernel(
     shards, owners, slot_count,
-    px_ref, raw_ref, ids_ref, wg_ref, wu_ref, wd_ref,
+    x_ref, g_ref, weight_ref, ids_ref, wg_ref, wu_ref, wd_ref,
     in_out, gg_out,
-    xbuf, gbuf, raw, packed, ids, wg, wu, wd, acc, factor, gg, strip, wide,
+    xbuf, gbuf, raw_own, raw, packed_x, packed, ids, wg, wu, wd, hidden, up, gate, gg, strip, wide,
     ids_send, ids_recv, swap_send, swap_recv, own_sem, ring_send, ring_recv,
     gg_send, gg_recv, load_sem, store_sem,
 ):
@@ -41,7 +41,7 @@
     place = ring_place(tok, shards)
     ahead = ring_index(place + 1, shards)
     behind = ring_index(place - 1, shards)
-    width = px_ref.shape[2]
+    width = x_ref.shape[1]
     full = xbuf.shape[2]
     cap = xbuf.shape[1]
     rows = shards * cap
@@ -81,7 +81,7 @@
         buf = (raw, xbuf)[a]
         half = buf.shape[2] // 2
         view = buf.at[block, :, pl.ds(c * half, half)]
-        src = raw_ref.at[:, pl.ds(c * half, half)] if a == 0 and hop == 0 else view
+        src = raw_own.at[:, pl.ds(c * half, half)] if a == 0 and hop == 0 else view
         copies[a, d, hop, c] = remote(
             src,
             view,
@@ -109,10 +109,13 @@
 
     slot_iota = lax.broadcasted_iota(jnp.int32, (owners * cap, ids.shape[2]), 0)
 
-    def pack(j, block, tokens):
-        picks = (slot_iota == ids[block, 0:1, :]).astype(jnp.float32).astype(jnp.bfloat16)
+    def choose(row, tokens):
+        picks = (slot_iota == row).astype(jnp.float32).astype(jnp.bfloat16)
         chosen = jnp.dot(picks, tokens, preferred_element_type=jnp.float32)
-        packed[block] = chosen.astype(jnp.bfloat16).reshape(owners, cap, width)
+        return chosen.astype(jnp.bfloat16).reshape(owners, cap, width)
+
+    def pack(j, block, row, tokens):
+        packed[block] = choose(row, tokens)
         swap(j, lambda e: packed.at[block, e], gbuf, block)
 
     id_copies = []
@@ -121,16 +124,17 @@
         [(0, h) for h in range(far)] + [(1, h) for h in range(near)],
         [(0, h) for h in range(near)] + [(1, h) for h in range(far)],
     )
+    raw_own[...] = (weight_ref[...] * g_ref[...].astype(jnp.float32)).astype(raw.dtype)
     for c in range(2):
         for d in range(2):
             send(0, d, 0, c)
-    ids[tok] = ids_ref[...]
     for k in range(1, shards):
         id_copies.append(remote(
             ids_ref, ids.at[tok], ids_send.at[k], ids_recv.at[k], (lax.rem(tok + k, shards), exp)
         ))
-    swap(0, lambda e: px_ref.at[e], xbuf, tok)
-    pack(1, tok, raw_ref[...])
+    packed_x[...] = choose(ids_ref[0:1, :], x_ref[...])
+    swap(0, lambda e: packed_x.at[e], xbuf, tok)
+    pack(1, tok, ids_ref[0:1, :], raw_own[...])
     number = 2
 
     loads = []
@@ -159,13 +163,13 @@
                 send(*(orders[d][s][0], d, orders[d][s][1], c))
         for d, hop in landed:
             block = ring_index(place - hop if d == 0 else place + hop, shards)
-            pack(number, block, raw[block])
+            pack(number, block, ids[block, 0:1, :], raw[block])
             number += 1
 
-    def product(weights, buf):
-        step = min(1024, full)
-        acc[...] = jnp.zeros_like(acc)
-
+    step = min(1024, full)
+    parts = full // step
+
+    def product(weights, buf, acc, low, high):
         def body(i, carry):
             part = pl.ds(pl.multiple_of(i * step, step), step)
             acc[...] += lax.dot_general(
@@ -176,22 +180,22 @@
             )
             return carry
 
-        lax.fori_loop(0, full // step, body, 0)
-
+        lax.fori_loop(low, high, body, 0)
+
+    for acc in (hidden, up, gate):
+        acc[...] = jnp.zeros_like(acc)
     for j, wait in swaps:
         if j > 0:
             wait()
     for load in loads:
         load.wait()
-    product(wd, gbuf)
-    factor[...] = acc[...]
+    product(wd, gbuf, hidden, 0, parts)
     for c in range(2):
         for d in range(2):
             copies[1, d, orders[d][-1][1], c].wait_recv()
-    product(wu, xbuf)
-    factor[...] = factor[...] * acc[...]
-    product(wg, xbuf)
-    gg[tok] = (factor[...] * silu_slope(acc[...])).astype(gg.dtype)
+        for weights, acc in ((wu, up), (wg, gate)):
+            product(weights, xbuf, acc, c * parts // 2, (c + 1) * parts // 2)
+    gg[tok] = (hidden[...] * up[...] * silu_slope(gate[...])).astype(gg.dtype)
 
     tile = min(512, full)
     tiles = full // tile
@@ -247,6 +251,27 @@
     store_gg.wait()
 
 
+def finish_kernel(slot_count, wide_ref, gg_ref, in_out, grad_out, sems):
+    strips = sems.shape[0]
+    rows = wide_ref.shape[0] // strips
+    copies = []
+    for i in range(strips):
+        part = pl.ds(i * rows, rows)
+        copy = pltpu.make_async_copy(wide_ref.at[part, :], in_out.at[part, :], sems.at[i])
+        copy.start()
+        copies.append(copy)
+    shards, units, slots = gg_ref.shape
+    total = lax.dot_general(
+        gg_ref[lax.axis_index("tok")],
+        gg_ref[...].reshape(shards * units, slots),
+        NT,
+        preferred_element_type=jnp.float32,
+    )
+    grad_out[...] = total / float(slot_count)
+    for copy in copies:
+        copy.wait()
+
+
 def local(tokens_x, out_grad, expert_ids, route_q, gate_w, up_w, down_w):
     owners = lax.axis_size("exp")
     shards = lax.axis_size("tok")
@@ -263,12 +288,6 @@
     earlier = (fitted_id[:, None] == fitted_id[None, :]) & (order[:, None] > order[None, :])
     rank_in = jnp.sum(earlier.astype(jnp.int32), axis=1)
     slot_ids = fitted_id * padded + rank_in
-    packer = (slot_ids[None, :] == jnp.arange(owners * padded, dtype=jnp.int32)[:, None]).astype(
-        jnp.bfloat16
-    )
-    scaled = (route_weight[:, None] * out_grad.astype(jnp.float32)).astype(jnp.bfloat16)
-    packed_x = jnp.dot(packer, tokens_x, preferred_element_type=jnp.float32).astype(jnp.bfloat16)
-    packed_x = packed_x.reshape(owners, padded, local_width)
     id_rows = jnp.broadcast_to(slot_ids[None, :], (8, tok_rows))
     full_width = local_width * owners
     units = gate_w.shape[1]
@@ -277,23 +296,26 @@
     vmem = pl.BlockSpec(memory_space=pltpu.VMEM)
     anywhere = pl.BlockSpec(memory_space=pl.ANY)
     dma = pltpu.SemaphoreType.DMA
-    input_rows, gg_all = pl.pallas_call(
+    wide, gg_all = pl.pallas_call(
         functools.partial(exchange_kernel, shards, owners, slot_count),
         out_shape=(
             jax.ShapeDtypeStruct((full_width // shards, full_width), jnp.float32),
             jax.ShapeDtypeStruct((shards, units, rows), jnp.bfloat16),
         ),
-        in_specs=[vmem, vmem, vmem, anywhere, anywhere, anywhere],
+        in_specs=[vmem, vmem, vmem, vmem, anywhere, anywhere, anywhere],
         out_specs=(anywhere, anywhere),
         scratch_shapes=[
             pltpu.VMEM((shards, padded, full_width), jnp.bfloat16),
             pltpu.VMEM((shards, padded, full_width), jnp.bfloat16),
+            pltpu.VMEM((tok_rows, local_width), jnp.bfloat16),
             pltpu.VMEM((shards, tok_rows, local_width), jnp.bfloat16),
+            pltpu.VMEM((owners, padded, local_width), jnp.bfloat16),
             pltpu.VMEM((shards, owners, padded, local_width), jnp.bfloat16),
             pltpu.VMEM((shards, 8, tok_rows), jnp.int32),
             pltpu.VMEM((units, full_width), jnp.bfloat16),
             pltpu.VMEM((units, full_width), jnp.bfloat16),
             pltpu.VMEM((units, full_width), jnp.bfloat16),
+            pltpu.VMEM((units, rows), jnp.float32),
             pltpu.VMEM((units, rows), jnp.float32),
             pltpu.VMEM((units, rows), jnp.float32),
             pltpu.VMEM((shards, units, rows), jnp.bfloat16),
@@ -319,12 +341,18 @@
             bytes_accessed=20 * 2**20,
             transcendentals=units * rows,
         ),
-    )(packed_x, scaled, id_rows, gate_w[0], up_w[0], down_w[0])
-    grad_cols = lax.dynamic_index_in_dim(gg_all, position, 0, keepdims=False)
-    grad_rows = lax.dot_general(
-        grad_cols, gg_all.reshape(shards * units, rows), NT, preferred_element_type=jnp.float32
-    )
-    grad_rows = grad_rows / float(slot_count)
+    )(tokens_x, out_grad, route_weight[:, None], id_rows, gate_w[0], up_w[0], down_w[0])
+    input_rows, grad_rows = pl.pallas_call(
+        functools.partial(finish_kernel, slot_count),
+        out_shape=(
+            jax.ShapeDtypeStruct((full_width // shards, full_width), jnp.float32),
+            jax.ShapeDtypeStruct((units, shards * units), jnp.float32),
+        ),
+        in_specs=[anywhere, vmem],
+        out_specs=(anywhere, vmem),
+        scratch_shapes=[dma((8,))],
+        compiler_params=pltpu.CompilerParams(vmem_limit_bytes=56 * 2**20),
+    )(wide, gg_all)
     return (input_rows[None], grad_rows[None])
 
 

time: 135 us -> 377 us (2.79)
  Pallas kernels: 118 us -> 374 us
  local copies, waits for them, and re-layouts: 8.39 us -> 1.36 us
  matrix products: 4.7 us -> 0 us
    pallas_call x0 -> x1, Pallas kernels: none -> 258 us  [local(): pl.pallas_call(functools.partial(finish_kernel, slot_count), out_shape=(j...]
    unnamed x3 -> x0, local copies, waits for them, and re-layouts: 7.79 us -> none
    dot_general x2 -> x0, matrix products: 4.7 us -> none  [the longest x1 3.53 us: local(): lax.dot_general(grad_cols, gg_all.reshape(shards * units, rows), NT, pref...]
where the time goes in v3:
time: 377 us
  Pallas kernels  374 us (99%)
    pallas_call x1, Pallas kernels, local(): pl.pallas_call(functools.partial(finish_kernel, slot_count), out_shape=(j...  258 us
    pallas_call x1, Pallas kernels, local(): pl.pallas_call(functools.partial(exchange_kernel, shards, owners, slot_co...  116 us

profile of v3, /device:TPU:0, one launch (start us, length us, event | category | flops | bytes accessed | tf_op | source)
XLA Modules:
  0.0 376.7 jit_solution(14272554530151961460)
XLA Ops:
  0.6 0.7 fusion.2
  1.4 0.2 convert_reduce_fusion
  1.6 0.6 broadcast_in_dim.12.ids_ref
  2.2 0.8 copy.10.weight_ref
  2.9 116.0 %shard_map.86 = (f32[512,4096]{1,0:T(8,128)}, bf16[8,192,640]{2,1,0:T(8,128)(2,1)}) custom-call(bf16[160,1024]{1,0:T(8,128)(2,1)} %x_ref.1, bf16[160,1024]{1,0:T(8,128)(2,1)} %g_ref.1, f32[160,1]{1,0:T(8,128)} %copy.10.weight_ref, s32[8,160]{1,0:T(8,128)} %broadcast_in_dim.12.ids_ref, bf16[192,4096]{1,0:T(8,128)(2,1)} %bitcast.8, bf16[192,4096]{1,0:T(8,128)(2,1)} %bitcast.9, ...), custom_call_target="tpu_custom_call" | custom-call | flops 3019898880 | bytes 20971520 | tf_op jit(solution)/shard_map/pallas_call | solution.py:299
  118.9 257.8 %shard_map.87 = (f32[512,4096]{1,0:T(8,128)}, f32[192,1536]{1,0:T(8,128)}) custom-call(f32[512,4096]{1,0:T(8,128)} %get-tuple-element.6.wide_ref, bf16[8,192,640]{2,1,0:T(8,128)(2,1)} %get-tuple-element.7.gg_ref), custom_call_target="tpu_custom_call" | custom-call | tf_op jit(solution)/shard_map/pallas_call | solution.py:345
  (2 shorter events, 0.0 us)

commit v4 on v3

--- a/solution.py
+++ b/solution.py
@@ -251,15 +251,19 @@
     store_gg.wait()
 
 
-def finish_kernel(slot_count, wide_ref, gg_ref, in_out, grad_out, sems):
-    strips = sems.shape[0]
+def finish_kernel(slot_count, wide_ref, gg_ref, in_out, grad_out, held, load_sems, store_sems):
+    strips = load_sems.shape[0]
     rows = wide_ref.shape[0] // strips
-    copies = []
+    loads, stores = [], []
     for i in range(strips):
         part = pl.ds(i * rows, rows)
-        copy = pltpu.make_async_copy(wide_ref.at[part, :], in_out.at[part, :], sems.at[i])
-        copy.start()
-        copies.append(copy)
+        load = pltpu.make_async_copy(wide_ref.at[part, :], held.at[part, :], load_sems.at[i])
+        load.start()
+        loads.append(load)
+        stores.append(pltpu.make_async_copy(held.at[part, :], in_out.at[part, :], store_sems.at[i]))
+    for load, store in zip(loads, stores):
+        load.wait()
+        store.start()
     shards, units, slots = gg_ref.shape
     total = lax.dot_general(
         gg_ref[lax.axis_index("tok")],
@@ -268,8 +272,8 @@
         preferred_element_type=jnp.float32,
     )
     grad_out[...] = total / float(slot_count)
-    for copy in copies:
-        copy.wait()
+    for store in stores:
+        store.wait()
 
 
 def local(tokens_x, out_grad, expert_ids, route_q, gate_w, up_w, down_w):
@@ -350,7 +354,11 @@
         ),
         in_specs=[anywhere, vmem],
         out_specs=(anywhere, vmem),
-        scratch_shapes=[dma((8,))],
+        scratch_shapes=[
+            pltpu.VMEM((full_width // shards, full_width), jnp.float32),
+            dma((8,)),
+            dma((8,)),
+        ],
         compiler_params=pltpu.CompilerParams(vmem_limit_bytes=56 * 2**20),
     )(wide, gg_all)
     return (input_rows[None], grad_rows[None])

time: 377 us -> 128 us (0.34)
  Pallas kernels: 374 us -> 125 us
    pallas_call x1, Pallas kernels: 258 us -> 8.98 us  [local(): pl.pallas_call(functools.partial(finish_kernel, slot_count), out_shape=(j...]
where the time goes in v4:
time: 128 us
  Pallas kernels  125 us (98%)
  local copies, waits for them, and re-layouts  1.36 us (1%)
    pallas_call x1, Pallas kernels, local(): pl.pallas_call(functools.partial(exchange_kernel, shards, owners, slot_co...  116 us
    pallas_call x1, Pallas kernels, local(): pl.pallas_call(functools.partial(finish_kernel, slot_count), out_shape=(j...  8.98 us

profile of v4, /device:TPU:0, one launch (start us, length us, event | category | flops | bytes accessed | tf_op | source)
XLA Modules:
  0.0 127.9 jit_solution(5108880459087233493)
XLA Ops:
  0.6 0.7 fusion.2
  1.4 0.2 convert_reduce_fusion
  1.6 0.6 broadcast_in_dim.12.ids_ref
  2.2 0.8 copy.10.weight_ref
  2.9 116.0 %shard_map.86 = (f32[512,4096]{1,0:T(8,128)}, bf16[8,192,640]{2,1,0:T(8,128)(2,1)}) custom-call(bf16[160,1024]{1,0:T(8,128)(2,1)} %x_ref.1, bf16[160,1024]{1,0:T(8,128)(2,1)} %g_ref.1, f32[160,1]{1,0:T(8,128)} %copy.10.weight_ref, s32[8,160]{1,0:T(8,128)} %broadcast_in_dim.12.ids_ref, bf16[192,4096]{1,0:T(8,128)(2,1)} %bitcast.8, bf16[192,4096]{1,0:T(8,128)(2,1)} %bitcast.9, ...), custom_call_target="tpu_custom_call" | custom-call | flops 3019898880 | bytes 20971520 | tf_op jit(solution)/shard_map/pallas_call | solution.py:303
  118.9 9.0 %shard_map.87 = (f32[512,4096]{1,0:T(8,128)}, f32[192,1536]{1,0:T(8,128)}) custom-call(f32[512,4096]{1,0:T(8,128)} %get-tuple-element.6.wide_ref, bf16[8,192,640]{2,1,0:T(8,128)(2,1)} %get-tuple-element.7.gg_ref), custom_call_target="tpu_custom_call" | custom-call | tf_op jit(solution)/shard_map/pallas_call | solution.py:349
  (2 shorter events, 0.0 us)
